TPU v7x, 32 devices: a whole 2x2x4 slice. The times are simulated.
32 devices in a mesh: seq: 8 (over z, core), head: 4 (over y, x).
Axes of the slice: x: 2, y: 2, z: 4, core: 2. Of those that a mesh axis runs over, the one named last changes fastest.
Arguments:
- queries: bfloat16 [1024, 2048], P('seq', 'head'), may hold values from -6 to 6
- key_value: bfloat16 [1024, 512], P('seq', 'head'), may hold values from -6 to 6
- grad_out: bfloat16 [1024, 2048], P('seq', 'head'), may hold values from -60 to 60
- ssm_grad: bfloat16 [1024, 2048], P('seq', 'head'), may hold values from -60 to 60
- b_proj: bfloat16 [1024, 128], P('seq'), may hold values from -1.5 to 1.5
- c_proj: bfloat16 [1024, 128], P('seq'), may hold values from -1.5 to 1.5
- decay_log: float32 [32, 1024], P('head', 'seq'), may hold values from -1.2 to 0
- skip_gain: float32 [32], P('head'), may hold values from 1 to 16
Outputs:
- grad_queries: bfloat16 [1024, 2048], P('seq', 'head')
- grad_key_value: bfloat16 [1024, 512], P('seq', 'head')
- grad_ssm_in: bfloat16 [1024, 2048], P('seq', 'head')
All inputs are finite; a program needn't handle non-finite values. Where the computation divides by a largest or mean magnitude, that divisor is 1e-20 or more.
Results may differ from a plain program's by a relative error of at most 0.012.
Values may be sent and summed in bfloat16 or wider, within the bound.
A program may use at most 64 MiB of HBM per device.

v0:
```python
import math

import jax
import jax.numpy as jnp
from jax import lax
from jax.sharding import PartitionSpec as P

epsilon = 1e-06
highest = lax.Precision.HIGHEST


def from_partner(block, axis, stride):
    count = lax.axis_size(axis)
    route = []
    for low in range(count):
        high = low | 1 << stride
        if high != low and high < count:
            route += [(low, high), (high, low)]
    return lax.ppermute(block, axis, route)


def carried_in(part, axis, combine, identity):
    count = lax.axis_size(axis)
    place = lax.axis_index(axis)
    ahead = count - 1 - place
    gathered = jax.tree.map(lambda a: lax.all_gather(a, axis), part)
    state = jax.tree.map(lambda a, e: jnp.zeros_like(a) + jnp.asarray(e, a.dtype), part, identity)

    def one(step, state):
        source = count - 1 - step
        return combine(
            state, jax.tree.map(lambda a: lax.dynamic_index_in_dim(a, source, 0, False), gathered)
        )

    return lax.fori_loop(0, ahead, one, state)


def pair_swap(values):
    return from_partner(values, "head", 0)


def chain_states(earlier_tokens, later):
    far_decay, far_state = earlier_tokens
    nearby_decay, near_state = later
    return (nearby_decay * far_decay, near_state + nearby_decay[:, None, None] * far_state)


def masked_probs(scores, visible, log_total):
    shifted = jnp.where(visible, scores - log_total, 0.0)
    return jnp.where(visible, jnp.exp(shifted), 0.0)


def on_device(queries, key_value, grad_out, ssm_grad, b_proj, c_proj, decay_log, skip_gain):
    tok_rows = queries.shape[0]
    head_size = key_value.shape[1]
    head_count = queries.shape[1] // head_size
    all_rows = tok_rows * lax.axis_size("seq")
    key_block = min(512, all_rows)
    block_count = all_rows // key_block
    score_scale = 1.0 / math.sqrt(head_size)
    parity = lax.axis_index("head") % 2
    partner = pair_swap(key_value.astype(jnp.float32)).astype(jnp.bfloat16)
    keys_own = jnp.where(parity == 0, key_value, partner)
    values_own = jnp.where(parity == 0, partner, key_value)
    key_rows_full, values_all = (
        lax.all_gather(keys_own, "seq", axis=0, tiled=True),
        lax.all_gather(values_own, "seq", axis=0, tiled=True),
    )
    key_blocks = key_rows_full.reshape(block_count, key_block, head_size)
    value_blocks = values_all.reshape(block_count, key_block, head_size)
    block_starts = jnp.arange(block_count, dtype=jnp.int32) * key_block
    query_three = queries.reshape(tok_rows, head_count, head_size)
    grad_three = grad_out.reshape(tok_rows, head_count, head_size)
    query_pos = lax.axis_index("seq") * tok_rows + jnp.arange(tok_rows, dtype=jnp.int32)

    def tile_logits(keys_blk, start):
        scores = (
            jnp.einsum("thd,sd->hts", query_three, keys_blk, preferred_element_type=jnp.float32)
            * score_scale
        )
        key_pos = start + jnp.arange(key_block, dtype=jnp.int32)
        visible = key_pos[None, :] <= query_pos[:, None]
        return (scores, visible[None])

    def softmax_stats(carry, items):
        running_max, running_total = carry
        keys_blk, start = items
        scores, visible = tile_logits(keys_blk, start)
        masked = jnp.where(visible, scores, -1e30)
        new_max = jnp.maximum(running_max, jnp.max(masked, axis=2, keepdims=True))
        weights = jnp.where(visible, jnp.exp(masked - new_max), 0.0)
        new_total = running_total * jnp.exp(running_max - new_max) + jnp.sum(
            weights, axis=2, keepdims=True
        )
        return ((new_max, new_total), None)

    start_max = jnp.full((head_count, tok_rows, 1), -1e30, jnp.float32)
    start_total = jnp.zeros((head_count, tok_rows, 1), jnp.float32)
    (final_max, final_total), _ = lax.scan(
        softmax_stats, (start_max, start_total), (key_blocks, block_starts)
    )
    log_total = final_max + jnp.log(final_total)

    def output_step(carry, items):
        keys_blk, values_blk, start = items
        scores, visible = tile_logits(keys_blk, start)
        probs_b = masked_probs(scores, visible, log_total).astype(jnp.bfloat16)
        return (
            carry
            + jnp.einsum("hts,sd->thd", probs_b, values_blk, preferred_element_type=jnp.float32),
            None,
        )

    out_full, _ = lax.scan(
        output_step,
        jnp.zeros((tok_rows, head_count, head_size), jnp.float32),
        (key_blocks, value_blocks, block_starts),
    )
    out_b = lax.optimization_barrier(out_full.astype(jnp.bfloat16))
    delta = jnp.sum(grad_three.astype(jnp.float32) * out_b.astype(jnp.float32), axis=2)
    delta_heads = delta.T[:, :, None]

    def gradient_step(carry, items):
        keys_blk, values_blk, start = items
        scores, visible = tile_logits(keys_blk, start)
        probs = masked_probs(scores, visible, log_total)
        probs_b = probs.astype(jnp.bfloat16)
        value_grad = jnp.einsum(
            "hts,thd->sd", probs_b, grad_three, preferred_element_type=jnp.float32
        )
        dprob = jnp.einsum(
            "thd,sd->hts", grad_three, values_blk, preferred_element_type=jnp.float32
        )
        dscore_b = (probs * (dprob - delta_heads)).astype(jnp.bfloat16)
        carry = (
            carry
            + jnp.einsum("hts,sd->thd", dscore_b, keys_blk, preferred_element_type=jnp.float32)
            * score_scale
        )
        key_grad = (
            jnp.einsum("hts,thd->sd", dscore_b, query_three, preferred_element_type=jnp.float32)
            * score_scale
        )
        return (carry, (key_grad, value_grad))

    query_grad, (key_grads, value_grads) = lax.scan(
        gradient_step,
        jnp.zeros((tok_rows, head_count, head_size), jnp.float32),
        (key_blocks, value_blocks, block_starts),
    )
    key_grad_all = key_grads.reshape(all_rows, head_size)
    value_grad_all = value_grads.reshape(all_rows, head_size)
    own_all = jnp.where(parity == 0, key_grad_all, value_grad_all)
    other_all = jnp.where(parity == 0, value_grad_all, key_grad_all)
    kv_grad = lax.psum_scatter(
        own_all + pair_swap(other_all), "seq", scatter_dimension=0, tiled=True
    )
    ssm_rows = ssm_grad.shape[0]
    ssm_count = decay_log.shape[0]
    ssm_size = ssm_grad.shape[1] // ssm_count
    grad_in = ssm_grad.reshape(ssm_rows, ssm_count, ssm_size).astype(jnp.float32)
    b_float = b_proj.astype(jnp.float32)
    c_float = c_proj.astype(jnp.float32)
    accumulated = jnp.cumsum(decay_log, axis=1)
    upper_mask = jnp.arange(ssm_rows)[None, :] >= jnp.arange(ssm_rows)[:, None]
    spans = accumulated[:, None, :] - accumulated[:, :, None]
    decay_weights = jnp.where(
        upper_mask[None], jnp.exp(jnp.where(upper_mask[None], spans, 0.0)), 0.0
    )
    pair_scores = jnp.einsum("tn,sn->ts", b_proj, c_proj, preferred_element_type=jnp.float32)
    local_part = jnp.einsum(
        "hts,shp->thp", decay_weights * pair_scores[None], grad_in, precision=highest
    )
    entry_decay = jnp.exp(accumulated)
    state_terms = jnp.einsum("sh,shp,sn->hpn", entry_decay.T, grad_in, c_float, precision=highest)
    decay_total = entry_decay[:, -1]
    _, incoming = carried_in(
        (decay_total, state_terms),
        "seq",
        chain_states,
        (jnp.ones_like(decay_total), jnp.zeros_like(state_terms)),
    )
    tail_decay = jnp.exp(accumulated[:, -1:] - accumulated)
    carried_part = (
        jnp.einsum("tn,hpn->thp", b_float, incoming, precision=highest) * tail_decay.T[:, :, None]
    )
    ssm_out = local_part + carried_part + skip_gain[None, :, None] * grad_in
    peak_q, peak_kv, peak_x = lax.pmax(
        (jnp.max(jnp.abs(query_grad)), jnp.max(jnp.abs(kv_grad)), jnp.max(jnp.abs(ssm_out))),
        ("seq", "head"),
    )
    query_flat = query_grad.reshape(tok_rows, head_count * head_size)
    flattened_statespace = ssm_out.reshape(ssm_rows, ssm_count * ssm_size)
    return (
        (query_flat / (peak_q + epsilon)).astype(jnp.bfloat16),
        (kv_grad / (peak_kv + epsilon)).astype(jnp.bfloat16),
        (flattened_statespace / (peak_x + epsilon)).astype(jnp.bfloat16),
    )


def solution(mesh):
    return jax.shard_map(
        on_device,
        mesh=mesh,
        in_specs=(
            P("seq", "head"),
            P("seq", "head"),
            P("seq", "head"),
            P("seq", "head"),
            P("seq", None),
            P("seq", None),
            P("head", "seq"),
            P("head"),
        ),
        out_specs=(P("seq", "head"), P("seq", "head"), P("seq", "head")),
        check_vma=False,
    )
```

profile of v0, /device:TPU:0, one launch (start us, length us, event | category | flops | bytes accessed | tf_op | source)
XLA Modules:
  0.0 193.7 jit_solution(10122019214012976585)
XLA Ops:
  7.2 3.0 %collective-permute-start = (bf16[128,128]{1,0:T(8,128)(2,1)}, bf16[128,128]{1,0:T(8,128)(2,1)S(1)}, u32[]{:S(2)}, u32[]{:S(2)}) collective-permute-start(bf16[128,128]{1,0:T(8,128)(2,1)} %param.17), channel_id=1, source_target_pairs={{0,1},{1,0},{2,3},{3,2},{4,5},{5,4},{6,7},{7,6},{8,9},{9,8},{10,11... | collective-permute-start | bytes 98312 | tf_op jit(solution)/shard_map/ppermute | solution.py:19
  10.3 1.0 copy.34
  11.4 1.0 copy.36
  12.6 0.8 broadcast_select_fusion.2
  13.4 14.7 %all_gather.15 = bf16[1024,128]{1,0:T(8,128)(2,1)S(1)} all-gather(bf16[128,128]{1,0:T(8,128)(2,1)S(1)} %get-tuple-element.480), channel_id=1, replica_groups=mesh['seq'=8,'head'=4] {'seq'}, dimensions={0}, use_global_device_ids=true | all-gather | bytes 294912 | tf_op jit(solution)/shard_map/all_gather | solution.py:66
  28.1 3.8 %while.54 = (s32[]{:T(128)}, f32[4,128,1]{1,0,2:T(4,128)S(1)}, f32[4,128,1]{1,0,2:T(4,128)S(1)}, s32[2]{0:T(128)S(1)}, bf16[2,512,128]{2,1,0:T(8,128)(2,1)S(1)},...) while((s32[]{:T(128)}, f32[4,128,1]{1,0,2:T(4,128)S(1)}, ...), condition=%wide.region_3.4_spmd.clone, body=%wide.region_0.3_spmd.clone.sunk | while | flops 68750464 | bytes 2587776 | solution.py:99
  28.1 0.6 dynamic_slice.93
  28.6 0.6 iota_add_fusion.13
  29.9 0.6 dynamic_slice.93
  31.8 14.2 %all_gather.16 = bf16[1024,128]{1,0:T(8,128)(2,1)S(1)} all-gather(bf16[128,128]{1,0:T(8,128)(2,1)S(1)} %get-tuple-element.479), channel_id=1, replica_groups=mesh['seq'=8,'head'=4] {'seq'}, dimensions={0}, use_global_device_ids=true | all-gather | bytes 294912 | tf_op jit(solution)/shard_map/all_gather | solution.py:67
  46.0 4.0 %while.55 = (s32[]{:T(128)}, f32[128,4,128]{0,2,1:T(8,128)S(1)}, bf16[2,512,128]{2,1,0:T(8,128)(2,1)S(1)}, s32[2]{0:T(128)S(1)}, bf16[2,512,128]{2,1,0:T(8,128)(...) while((s32[]{:T(128)}, f32[128,4,128]{0,2,1:T(8,128)S(1)}, ...), condition=%wide.region_5.6_spmd.clone, body=%wide.region_4.5_spmd.clone.sunk | while | flops 135725696 | bytes 1056899 | solution.py:114
  46.0 0.6 dynamic_slice.96
  46.6 0.6 iota_add_fusion.15
  47.4 0.6 fusion.116
  48.0 0.6 dynamic_slice.96
  48.6 0.6 iota_add_fusion.15
  49.4 0.6 fusion.116
  50.1 7.4 %while.56 = (s32[]{:T(128)}, f32[128,4,128]{0,2,1:T(8,128)S(1)}, f32[2,512,128]{2,1,0:T(8,128)S(1)}, f32[2,512,128]{2,1,0:T(8,128)}, bf16[2,512,128]{2,1,0:T(8,1...) while((s32[]{:T(128)}, f32[128,4,128]{0,2,1:T(8,128)S(1)}, ...), condition=%wide.region_8.9_spmd.clone, body=%wide.region_7.8_spmd.clone.sunk | while | flops 337969792 | bytes 6825651 | solution.py:146
  50.2 0.6 dynamic_slice.100
  50.7 0.6 iota_add_fusion.17
  52.8 1.0 fusion.131
  53.8 0.6 dynamic_slice.100
  54.4 0.6 iota_add_fusion.17
  56.5 1.0 fusion.131
  57.6 1.1 broadcast_select_fusion.1
  58.7 1.6 collective-permute-start.1
  60.3 12.7 %collective-permute-done.1 = f32[1024,128]{1,0:T(8,128)S(1)} collective-permute-done((f32[1024,128]{1,0:T(8,128)S(1)}, f32[1024,128]{1,0:T(8,128)S(1)}, u32[]{:S(2)}, u32[]{:S(2)}) %collective-permute-start.1) | collective-permute-done | bytes 524320 | tf_op jit(solution)/shard_map/ppermute | solution.py:19
  73.0 0.9 bitcast_add_fusion.2
  74.6 1.0 fusion.66
  75.6 0.6 dynamic-slice
  77.3 16.2 %all-reduce = f32[64]{0:T(128)S(1)} all-reduce(f32[64]{0:T(128)S(1)} %dynamic-update-slice), channel_id=3, replica_groups=mesh['seq'=8,'head'=4] {'seq'}, use_global_device_ids=true, to_apply=%add | all-reduce | flops 64 | bytes 512
  93.7 0.6 abs_reduce_fusion.1
  94.3 11.7 %reduce-scatter.2.cloned.1.call-done = f32[128,128]{1,0:T(8,128)} async-done(((f32[1024,128]{1,0:T(8,128)}), f32[128,128]{1,0:T(8,128)}) %reduce-scatter.2.cloned.1.call-update) | async-done | bytes 65552 | tf_op jit(solution)/shard_map/reduce_scatter | solution.py:155
  106.1 1.4 abs_reduce_fusion.2
  107.5 27.5 %all-gather.4.cloned.1.call-done = f32[64,64,128]{2,1,0:T(8,128)} async-done(((f32[8,64,128]{2,1,0:T(8,128)}), f32[64,64,128]{2,1,0:T(8,128)}) %all-gather.4.cloned.1.call-update) | async-done | bytes 2097168 | tf_op jit(solution)/shard_map/all_gather | solution.py:26
  135.0 7.8 %while.53 = (s32[]{:T(128)}, f32[8,64,128]{2,1,0:T(8,128)S(1)}, s32[]{:T(128)}, f32[8,8,64,128]{3,2,1,0:T(8,128)}, f32[8,8]{1,0:T(8,128)S(1)}, /*index=5*/s32[]{:T(128)}, s32[]{:T(128)}, s32[]{:T(128)}, s32[]{:T(128)}) while((s32[]{:T(128)}, f32[8,64,128]{2,1,0:T(8,128)S(1)}, s32[]{:T(128)}, f32[8,8,64,128]{3,2,1,0:T(8,128)}, ...), condition=%wide.region_16.17_spmd, body=%wide.region_15.16_spmd.sunk | while | flops 131078 | bytes 786675 | solution.py:35
  135.1 1.1 bitcast_add_fusion.5
  136.2 1.1 bitcast_add_fusion.5
  137.3 1.1 bitcast_add_fusion.5
  138.4 1.1 bitcast_add_fusion.5
  139.5 1.1 bitcast_add_fusion.5
  140.6 1.1 bitcast_add_fusion.5
  141.7 1.1 bitcast_add_fusion.5
  143.1 1.4 abs_reduce_fusion
  144.5 38.2 %all-reduce.1 = (f32[]{:T(128)}, f32[]{:T(128)}, f32[]{:T(128)}) all-reduce(f32[]{:T(128)} %abs_reduce_fusion.1, f32[]{:T(128)} %abs_reduce_fusion.2, f32[]{:T(128)} %get-tuple-element.484), channel_id=1, replica_groups=mesh['seq'=8,'head'=4] {'seq','head'}, use_global_device_ids=true, to_apply=%region_10.11 | all-reduce | flops 3 | bytes 24 | tf_op jit(solution)/shard_map/pmax | solution.py:188
  183.3 0.8 copy.43
  185.5 0.8 copy.47
  186.3 0.6 divide_convert_fusion.2
  (83 shorter events, 7.3 us)
Async XLA Ops:
  7.2 67.4 %copy-start = (bf16[128,128]{1,0:T(8,128)(2,1)S(1)}, bf16[128,128]{1,0:T(8,128)(2,1)}, u32[]{:S(2)}) copy-start(bf16[128,128]{1,0:T(8,128)(2,1)} %param.21) | copy-start | bytes 98308
  7.2 98.9 %reduce-scatter.2.cloned.1.call-start = ((), (), s32[]{:S(2)}) async-start(), calls=%async_computation.1 | async-start | bytes 589824 | tf_op jit(solution)/shard_map/reduce_scatter | solution.py:155
  7.2 5.4 %collective-permute-start = (bf16[128,128]{1,0:T(8,128)(2,1)}, bf16[128,128]{1,0:T(8,128)(2,1)S(1)}, u32[]{:S(2)}, u32[]{:S(2)}) collective-permute-start(bf16[128,128]{1,0:T(8,128)(2,1)} %param.17), channel_id=1, source_target_pairs={{0,1},{1,0},{2,3},{3,2},{4,5},{5,4},{6,7},{7,6},{8,9},{9,8},{10,11... | collective-permute-start | bytes 98312 | tf_op jit(solution)/shard_map/ppermute | solution.py:19
  57.5 16.3 %copy-start.2 = (bf16[128,512]{1,0:T(8,128)(2,1)S(1)}, bf16[128,512]{1,0:T(8,128)(2,1)}, u32[]{:S(2)}) copy-start(bf16[128,512]{1,0:T(8,128)(2,1)} %param.19) | copy-start | bytes 393220
  57.5 16.5 %copy-start.4 = (f32[8,128]{1,0:T(8,128)S(1)}, f32[8,128]{1,0:T(8,128)}, u32[]{:S(2)}) copy-start(f32[8,128]{1,0:T(8,128)} %param.22) | copy-start | bytes 12292
  57.6 18.0 %copy-start.6 = (u32[32]{0:T(128)S(1)}, u32[32]{0:T(128)}, u32[]{:S(2)}) copy-start(u32[32]{0:T(128)} %constant.121) | copy-start | bytes 388
  58.7 34.9 %copy-start.3 = (bf16[128,128]{1,0:T(8,128)(2,1)S(1)}, bf16[128,128]{1,0:T(8,128)(2,1)}, u32[]{:S(2)}) copy-start(bf16[128,128]{1,0:T(8,128)(2,1)} %param.20) | copy-start | bytes 98308
  58.7 14.2 %collective-permute-start.1 = (f32[1024,128]{1,0:T(8,128)S(1)}, f32[1024,128]{1,0:T(8,128)S(1)}, u32[]{:S(2)}, u32[]{:S(2)}) collective-permute-start(f32[1024,128]{1,0:T(8,128)S(1)} %bitcast.227), channel_id=1, source_target_pairs={{0,1},{1,0},{2,3},{3,2},{4,5},{5,4},{6,7},{7,6},{8,9},{9,8},{10,11... | collective-permute-start | bytes 1572872 | tf_op jit(solution)/shard_map/ppermute | solution.py:19
  73.8 61.2 %all-gather.4.cloned.1.call-start = ((), (), s32[]{:S(2)}) async-start(), calls=%async_computation.2 | async-start | bytes 2359296 | tf_op jit(solution)/shard_map/all_gather | solution.py:26
  135.0 8.1 %copy-start.5 = (f32[8]{0:T(128)S(1)}, f32[8]{0:T(128)}, u32[]{:S(2)}) copy-start(f32[8]{0:T(128)} %param.23) | copy-start | bytes 100
  142.8 43.5 %copy-start.1 = (f32[128,128]{1,0:T(8,128)S(1)}, f32[128,128]{1,0:T(8,128)}, u32[]{:S(2)}) copy-start(f32[128,128]{1,0:T(8,128)} %reduce-scatter.2.cloned.1.call-done) | copy-start | bytes 196612
Sparse Core Ops, SparseCore 0:
  74.0 32.0 reduce-scatter.1
  107.8 27.1 all-gather.3
where the time goes:
time: 195 us; the launch traced here: 194 us
  blocking collectives  83.2 us (43%)
  waiting for transfers between devices  51.9 us (27%)
  other arithmetic  18.4 us (9%)
  between operations  16.9 us (9%)
  matrix products  9.11 us (5%)
  local copies, waits for them, and re-layouts  8.88 us (5%)
  starting transfers between devices  4.65 us (2%)
    pmax x1, blocking collectives, on_device(): lax.pmax((jnp.max(jnp.abs(query_grad)), jnp.max(jnp.abs(kv_grad)), jnp.ma...  38.2 us
    all_gather x1, waiting for transfers between devices, carried_in(): gathered = jax.tree.map(lambda a: lax.all_gather(a, axis), part)  27.5 us
    unnamed x1, blocking collectives  16.2 us
    all_gather x1, blocking collectives, on_device(): lax.all_gather(keys_own, 'seq', axis=0, tiled=True)  14.7 us
    all_gather x1, blocking collectives, on_device(): lax.all_gather(values_own, 'seq', axis=0, tiled=True)  14.2 us
    ppermute x2, waiting for transfers between devices, from_partner(): return lax.ppermute(block, axis, route)  12.7 us
    reduce_scatter x1, waiting for transfers between devices, on_device(): lax.psum_scatter(own_all + pair_swap(other_all), 'seq', scatter_dimension...  11.7 us
    add x7, other arithmetic, chain_states(): near_state + nearby_decay[:, None, None] * far_state  7.43 us
  transfers between devices with their start and end apart: 4, of which 3 were waited for; matrix products, arithmetic and copies ran while one was open for 4% of the time, Pallas kernels for 0%

commit v1 on v0

v1 whole, which is shorter than its diff:
```python
import functools
import math

import jax
import jax.numpy as jnp
from jax import lax
from jax.experimental import pallas as pl
from jax.experimental.pallas import tpu as pltpu
from jax.sharding import PartitionSpec as P

epsilon = 1e-06
f32 = jnp.float32
bf16 = jnp.bfloat16
MESH = pl.DeviceIdType.MESH


def nn(a, b):
    return jnp.dot(a, b, preferred_element_type=f32)


def nt(a, b, precision=None):
    return lax.dot_general(
        a, b, (((1,), (1,)), ((), ())), preferred_element_type=f32, precision=precision
    )


def kernel(
    n, hn, q_ref, kv_ref, do_ref, dy_ref, b_ref, c_ref, dl_ref, sg_ref,
    gq_ref, gkv_ref, gx_ref,
    kv_all, q_st, q_t, do_st, do_t, score, dkv_out, dkv_in,
    st_out, st_in, dt_out, dt_in, inc_out, inc_in, dx, am_out, am_in, am2_out, am2_in,
    kvs, kvr, dks, dkr, sts, str_, dts, dtr, ins, inr, ams, amr, am2s, am2r,
):
    s = lax.axis_index("seq")
    h = lax.axis_index("head")
    parity = lax.rem(h, 2)
    base = h - parity
    mate = base + 1 - parity
    rows, hd = kv_ref.shape
    heads = q_ref.shape[1] // hd
    cols = heads * rows
    scale = 1.0 / math.sqrt(hd)
    nh, srows = st_out.shape[:2]
    ssm_heads = dl_ref.shape[0]
    width = dy_ref.shape[1]
    sp = width // ssm_heads
    per = hd // sp
    chunk = 2 * rows

    barrier = pltpu.get_barrier_semaphore()

    @pl.loop(0, n)
    def _(d):
        pl.semaphore_signal(barrier, inc=1, device_id=(d, mate), device_id_type=MESH)

        @pl.when(d != s)
        def _():
            pl.semaphore_signal(barrier, inc=1, device_id=(d, h), device_id_type=MESH)

    @pl.loop(0, hn)
    def _(g):
        @pl.when(jnp.logical_and(g != h, g != mate))
        def _():
            pl.semaphore_signal(barrier, inc=1, device_id=(s, g), device_id_type=MESH)

    kv_all[parity, s] = kv_ref[...]

    @pl.when(jnp.logical_and(lax.rem(s, 2) == 0, s + 1 < n))
    def _():
        kv_all[0, s + 1] = jnp.zeros((rows, hd), bf16)
        kv_all[1, s + 1] = jnp.zeros((rows, hd), bf16)

    row_i = lax.broadcasted_iota(jnp.int32, (rows, rows), 0)
    col_i = lax.broadcasted_iota(jnp.int32, (rows, rows), 1)
    tril = jnp.where(col_i <= row_i, 1.0, 0.0).astype(f32)
    decay = dl_ref[...]
    cum = nt(decay, tril, lax.Precision.HIGHEST)
    cum_t = nt(tril, decay, lax.Precision.HIGHEST)
    lane = lax.broadcasted_iota(jnp.int32, (1, hd), 1) // sp

    def spread(x):
        parts = []
        for i in range(ssm_heads // per):
            v = x[:, i * per : i * per + 1]
            for k in range(1, per):
                v = jnp.where(lane == k, x[:, i * per + k : i * per + k + 1], v)
            parts.append(jnp.broadcast_to(v, (x.shape[0], hd)))
        return jnp.concatenate(parts, axis=1)

    dy = dy_ref[...]
    entry = spread(jnp.exp(cum_t))
    scaled = (dy.astype(f32) * entry).astype(bf16)
    c_val = c_ref[...]
    state_t = nn(c_val.T, scaled).astype(bf16)
    for j in range(nh):
        st_out[j] = state_t[j * srows : (j + 1) * srows]
    dt_out[...] = jnp.broadcast_to(jnp.exp(cum[:, rows - 1 : rows]), dt_out.shape)

    pl.semaphore_wait(barrier, 2 * n - 1 + hn - 2)

    def kv_copy(d, g, source, kind):
        return pltpu.make_async_remote_copy(
            src_ref=kv_ref, dst_ref=kv_all.at[kind, source],
            send_sem=kvs.at[g - base, d], recv_sem=kvr.at[kind, source],
            device_id=(d, g), device_id_type=MESH,
        )

    def st_copy(j, source):
        return pltpu.make_async_remote_copy(
            src_ref=st_out.at[j], dst_ref=st_in.at[source],
            send_sem=sts.at[j], recv_sem=str_.at[source],
            device_id=(j, h), device_id_type=MESH,
        )

    def dt_copy(j, source):
        return pltpu.make_async_remote_copy(
            src_ref=dt_out, dst_ref=dt_in.at[source],
            send_sem=dts.at[j], recv_sem=dtr.at[source],
            device_id=(j, h), device_id_type=MESH,
        )

    def inc_copy(d, source):
        return pltpu.make_async_remote_copy(
            src_ref=inc_out.at[d], dst_ref=inc_in.at[source],
            send_sem=ins.at[d], recv_sem=inr.at[source],
            device_id=(d, h), device_id_type=MESH,
        )

    kv_copy(s, mate, s, parity).start()

    @pl.loop(0, nh)
    def _(j):
        @pl.when(j != s)
        def _():
            dt_copy(j, s).start()
            st_copy(j, s).start()

    @pl.loop(s + 1, n)
    def _(d):
        kv_copy(d, h, s, parity).start()
        kv_copy(d, mate, s, parity).start()

    for i in range(heads):
        q_i = q_ref[:, i * hd : (i + 1) * hd]
        d_i = do_ref[:, i * hd : (i + 1) * hd]
        q_st[i * rows : (i + 1) * rows] = q_i
        do_st[i * rows : (i + 1) * rows] = d_i
        q_t[:, i * rows : (i + 1) * rows] = q_i.T
        do_t[:, i * rows : (i + 1) * rows] = d_i.T

    pair = nt(b_ref[...], c_val)
    upper = col_i >= row_i
    for i in range(ssm_heads // per):
        dy_i = dy[:, i * hd : (i + 1) * hd]
        total = None
        gain = None
        for k in range(per):
            a = i * per + k
            span = jnp.where(upper, cum[a : a + 1, :] - cum_t[:, a : a + 1], -1e30)
            w = (jnp.exp(span) * pair).astype(bf16)
            r = nn(w, dy_i)
            total = r if k == 0 else jnp.where(lane == k, r, total)
            gain = (
                jnp.full((1, hd), sg_ref[a], f32) if k == 0 else jnp.where(lane == k, sg_ref[a], gain)
            )
        dx[:, i * hd : (i + 1) * hd] = total + gain * dy_i.astype(f32)

    @pl.when(s < nh)
    def _():
        st_in[s] = st_out[jnp.minimum(s, nh - 1)]
        dt_in[s] = dt_out[...]

        def one(step, inc):
            i = n - 1 - step
            inc_out[i] = inc.astype(bf16)

            @pl.when(i != s)
            def _():
                inc_copy(i, s).start()
                st_copy(jnp.minimum(s, nh - 1), i).wait_recv()
                dt_copy(jnp.minimum(s, nh - 1), i).wait_recv()

            d = dt_in[i]
            parts = []
            for a in range(ssm_heads // per):
                v = d[a * per : a * per + 1]
                for k in range(1, per):
                    v = jnp.where(lane == k, d[a * per + k : a * per + k + 1], v)
                parts.append(v)
            return st_in[i].astype(f32) + jnp.concatenate(parts, axis=1) * inc

        lax.fori_loop(0, n, one, jnp.zeros((srows, width), f32))
        inc_in[jnp.minimum(s, nh - 1)] = inc_out[s]

    chunks = s // 2 + 1
    key_i = lax.broadcasted_iota(jnp.int32, (chunk, cols), 0)
    query_i = s * rows + lax.rem(lax.broadcasted_iota(jnp.int32, (1, cols), 1), rows)

    def await_kind(kind, j):
        for k in range(2):
            blk = 2 * j + k

            @pl.when(jnp.logical_and(blk <= s, jnp.logical_or(blk != s, parity != kind)))
            def _():
                kv_copy(s, h, blk, kind).wait_recv()

    def load(kind, j):
        return kv_all[kind, pl.ds(2 * j, 2)].reshape(chunk, hd)

    def first(j, top):
        await_kind(0, j)
        sc = nn(load(0, j), q_t[...]) * scale
        sc = jnp.where(key_i + j * chunk <= query_i, sc, -1e30)
        score[j] = sc
        return jnp.maximum(top, jnp.max(sc, axis=0, keepdims=True))

    top = lax.fori_loop(0, chunks, first, jnp.full((1, cols), -1e30, f32))

    def second(j, total):
        e = jnp.exp(score[j] - top)
        score[j] = e
        return total + jnp.sum(e, axis=0, keepdims=True)

    total = lax.fori_loop(0, chunks, second, jnp.zeros((1, cols), f32))
    inv = 1.0 / total

    def dkv_copy(kind, blk, source, member):
        return pltpu.make_async_remote_copy(
            src_ref=dkv_out.at[kind, blk], dst_ref=dkv_in.at[source, member],
            send_sem=dks.at[kind, blk], recv_sem=dkr.at[source, member],
            device_id=(blk, base + kind), device_id_type=MESH,
        )

    def other(kind, blk):
        return jnp.logical_and(blk <= s, jnp.logical_or(blk != s, parity != kind))

    def send_grads(kind, j, val):
        for k in range(2):
            blk = 2 * j + k
            dkv_out[kind, blk] = val[k * rows : (k + 1) * rows].astype(bf16)

            @pl.when(other(kind, blk))
            def _():
                dkv_copy(kind, blk, s, parity).start()

    def third(j, out):
        await_kind(1, j)
        p = score[j] * inv
        score[j] = p
        pb = p.astype(bf16)
        send_grads(1, j, nn(pb, do_st[...]))
        return out + nn(load(1, j).T, pb)

    out_t = lax.fori_loop(0, chunks, third, jnp.zeros((hd, cols), f32))
    delta = jnp.sum(do_t[...].astype(f32) * out_t.astype(bf16).astype(f32), axis=0, keepdims=True)

    def fourth(j, dq):
        dp = nn(load(1, j), do_t[...])
        ds = (score[j] * (dp - delta)).astype(bf16)
        send_grads(0, j, nn(ds, q_st[...]) * scale)
        return dq + nn(load(0, j).T, ds)

    dq_t = lax.fori_loop(0, chunks, fourth, jnp.zeros((hd, cols), f32)) * scale

    @pl.loop(0, nh)
    def _(j):
        @pl.when(j != s)
        def _():
            inc_copy(s, j).wait_recv()

    carried = nn(b_ref[...], inc_in[...].reshape(nh * srows, width))
    tail = spread(jnp.exp(cum_t[rows - 1 : rows, :] - cum_t))
    dx_full = dx[...] + carried * tail
    dx[...] = dx_full

    def peak(x):
        return jnp.max(jnp.max(jnp.abs(x), axis=0, keepdims=True), axis=1, keepdims=True)

    peak_q = peak(dq_t)
    peak_x = peak(dx_full)

    def add_source(i, acc):
        for m in range(2):
            @pl.when(jnp.logical_or(i != s, parity != m))
            def _():
                dkv_copy(parity, s, i, m).wait_recv()

            acc = acc + dkv_in[i, m].astype(f32)
        return acc

    dkv_in[s, parity] = dkv_out[parity, s]
    kv_grad = lax.fori_loop(s, n, add_source, jnp.zeros((rows, hd), f32))
    peak_kv = peak(kv_grad)

    sub = lax.broadcasted_iota(jnp.int32, am_out.shape, 0)
    mine = jnp.where(sub == 0, peak_q, jnp.where(sub == 1, peak_kv, peak_x))
    am_out[...] = mine
    am_in[s] = mine

    def am_copy(d, source):
        return pltpu.make_async_remote_copy(
            src_ref=am_out, dst_ref=am_in.at[source],
            send_sem=ams.at[d], recv_sem=amr.at[source],
            device_id=(d, h), device_id_type=MESH,
        )

    def am2_copy(g, source):
        return pltpu.make_async_remote_copy(
            src_ref=am2_out, dst_ref=am2_in.at[source],
            send_sem=am2s.at[g], recv_sem=am2r.at[source],
            device_id=(s, g), device_id_type=MESH,
        )

    def each_other(count, me, act):
        @pl.loop(0, count)
        def _(d):
            @pl.when(d != me)
            def _():
                act(d)

    each_other(n, s, lambda d: am_copy(d, s).start())
    each_other(n, s, lambda d: am_copy(s, d).wait_recv())
    column = jnp.max(am_in[...], axis=0)
    am2_out[...] = column
    am2_in[h] = column
    each_other(hn, h, lambda g: am2_copy(g, h).start())
    each_other(hn, h, lambda g: am2_copy(h, g).wait_recv())
    inverse = 1.0 / (jnp.max(am2_in[...], axis=0) + epsilon)

    scaled_q = dq_t * inverse[0:1, 0:1]
    for i in range(heads):
        gq_ref[:, i * hd : (i + 1) * hd] = scaled_q[:, i * rows : (i + 1) * rows].T.astype(bf16)
    gkv_ref[...] = (kv_grad * inverse[1:2, 0:1]).astype(bf16)
    gx_ref[...] = (dx[...] * inverse[2:3, 0:1]).astype(bf16)

    kv_copy(s, mate, s, parity).wait_send()

    @pl.loop(s + 1, n)
    def _(d):
        kv_copy(d, h, s, parity).wait_send()
        kv_copy(d, mate, s, parity).wait_send()

    @pl.loop(0, nh)
    def _(j):
        @pl.when(j != s)
        def _():
            st_copy(j, s).wait_send()
            dt_copy(j, s).wait_send()

    @pl.when(s < nh)
    def _():
        each_other(n, s, lambda d: inc_copy(d, s).wait_send())

    @pl.loop(0, s + 1)
    def _(blk):
        for kind in range(2):
            @pl.when(other(kind, blk))
            def _():
                dkv_copy(kind, blk, s, parity).wait_send()

    each_other(n, s, lambda d: am_copy(d, s).wait_send())
    each_other(hn, h, lambda g: am2_copy(g, h).wait_send())


def on_device(queries, key_value, grad_out, ssm_grad, b_proj, c_proj, decay_log, skip_gain):
    n = lax.axis_size("seq")
    hn = lax.axis_size("head")
    rows, hd = key_value.shape
    heads = queries.shape[1] // hd
    cols = heads * rows
    width = ssm_grad.shape[1]
    state = b_proj.shape[1]
    ssm_heads = decay_log.shape[0]
    nh = min(n, state // 16)
    srows = state // nh
    vmem = pltpu.VMEM
    dma = pltpu.SemaphoreType.DMA
    full = pl.BlockSpec(memory_space=pltpu.VMEM)
    return pl.pallas_call(
        functools.partial(kernel, n, hn),
        out_shape=(
            jax.ShapeDtypeStruct(queries.shape, bf16),
            jax.ShapeDtypeStruct(key_value.shape, bf16),
            jax.ShapeDtypeStruct(ssm_grad.shape, bf16),
        ),
        in_specs=[full] * 7 + [pl.BlockSpec(memory_space=pltpu.SMEM)],
        out_specs=(full, full, full),
        scratch_shapes=[
            vmem((2, n, rows, hd), bf16),
            vmem((cols, hd), bf16),
            vmem((hd, cols), bf16),
            vmem((cols, hd), bf16),
            vmem((hd, cols), bf16),
            vmem((n // 2, 2 * rows, cols), f32),
            vmem((2, n, rows, hd), bf16),
            vmem((n, 2, rows, hd), bf16),
            vmem((nh, srows, width), bf16),
            vmem((n, srows, width), bf16),
            vmem((ssm_heads, hd), f32),
            vmem((n, ssm_heads, hd), f32),
            vmem((n, srows, width), bf16),
            vmem((nh, srows, width), bf16),
            vmem((rows, width), f32),
            vmem((8, hd), f32),
            vmem((n, 8, hd), f32),
            vmem((8, hd), f32),
            vmem((hn, 8, hd), f32),
            dma((2, n)), dma((2, n)),
            dma((2, n)), dma((n, 2)),
            dma((nh,)), dma((n,)),
            dma((nh,)), dma((n,)),
            dma((n,)), dma((nh,)),
            dma((n,)), dma((n,)),
            dma((hn,)), dma((hn,)),
        ],
        compiler_params=pltpu.CompilerParams(
            collective_id=0, has_side_effects=True, vmem_limit_bytes=48 * 1024 * 1024
        ),
    )(queries, key_value, grad_out, ssm_grad, b_proj, c_proj, decay_log, skip_gain)


def solution(mesh):
    return jax.shard_map(
        on_device,
        mesh=mesh,
        in_specs=(
            P("seq", "head"),
            P("seq", "head"),
            P("seq", "head"),
            P("seq", "head"),
            P("seq", None),
            P("seq", None),
            P("head", "seq"),
            P("head"),
        ),
        out_specs=(P("seq", "head"), P("seq", "head"), P("seq", "head")),
        check_vma=False,
    )
```

time: 195 us -> 54 us (0.28)
  blocking collectives: 83.2 us -> 0 us
  waiting for transfers between devices: 51.9 us -> 0 us
  Pallas kernels: 0 us -> 44.6 us
  other arithmetic: 18.4 us -> 0 us
  between operations: 16.9 us -> 0.66 us
  matrix products: 9.11 us -> 0 us
  starting transfers between devices: 4.65 us -> 0 us
    pallas_call x0 -> x1, Pallas kernels: none -> 44.6 us  [on_device(): pl.pallas_call(functools.partial(kernel, n, hn), out_shape=(jax.ShapeDtyp...]
    pmax x1 -> x0, blocking collectives: 38.2 us -> none  [on_device(): lax.pmax((jnp.max(jnp.abs(query_grad)), jnp.max(jnp.abs(kv_grad)), jnp.ma...]
    all_gather x2 -> x0, blocking collectives: 28.9 us -> none  [the longest x1 14.7 us: on_device(): lax.all_gather(keys_own, 'seq', axis=0, tiled=True)]
    all_gather x1 -> x0, waiting for transfers between devices: 27.5 us -> none  [carried_in(): gathered = jax.tree.map(lambda a: lax.all_gather(a, axis), part)]
    unnamed x1 -> x0, blocking collectives: 16.2 us -> none
    ppermute x2 -> x0, waiting for transfers between devices: 12.7 us -> none  [from_partner(): return lax.ppermute(block, axis, route)]
    add x23 -> x0, other arithmetic: 12.1 us -> none  [the longest x7 7.43 us: chain_states(): near_state + nearby_decay[:, None, None] * far_state]
    reduce_scatter x1 -> x0, waiting for transfers between devices: 11.7 us -> none  [on_device(): lax.psum_scatter(own_all + pair_swap(other_all), 'seq', scatter_dimension...]
  transfers between devices with their start and end apart: 4 -> 0, of which waited for: 3 -> 0; matrix products, arithmetic and copies ran while one was open for 4% -> 0% of each run, Pallas kernels for 0% -> 0%
where the time goes in v1:
time: 54 us; the launch traced here: 53.6 us
  Pallas kernels  44.6 us (83%)
  local copies, waits for them, and re-layouts  8.24 us (15%)
  between operations  0.66 us (1%)
    pallas_call x1, Pallas kernels, on_device(): pl.pallas_call(functools.partial(kernel, n, hn), out_shape=(jax.ShapeDtyp...  44.6 us
    unnamed x19, local copies, waits for them, and re-layouts  8.24 us

profile of v1, /device:TPU:0, one launch (start us, length us, event | category | flops | bytes accessed | tf_op | source)
XLA Modules:
  0.0 53.6 jit_solution(5478053588385860629)
XLA Ops:
  0.6 0.0 copy-start
  0.6 0.9 %copy-done = bf16[128,512]{1,0:T(8,128)(2,1)S(1)} copy-done((bf16[128,512]{1,0:T(8,128)(2,1)S(1)}, bf16[128,512]{1,0:T(8,128)(2,1)}, u32[]{:S(2)}) %copy-start) | copy-done | bytes 131096
  1.5 0.0 copy-start.1
  1.5 0.9 %copy-done.1 = bf16[128,512]{1,0:T(8,128)(2,1)S(1)} copy-done((bf16[128,512]{1,0:T(8,128)(2,1)S(1)}, bf16[128,512]{1,0:T(8,128)(2,1)}, u32[]{:S(2)}) %copy-start.1) | copy-done | bytes 131096
  2.4 0.0 copy-start.2
  2.4 0.9 %copy-done.2 = bf16[128,512]{1,0:T(8,128)(2,1)S(1)} copy-done((bf16[128,512]{1,0:T(8,128)(2,1)S(1)}, bf16[128,512]{1,0:T(8,128)(2,1)}, u32[]{:S(2)}) %copy-start.2) | copy-done | bytes 131096
  3.3 0.0 copy-start.3
  3.4 0.8 %copy-done.3 = bf16[128,128]{1,0:T(8,128)(2,1)S(1)} copy-done((bf16[128,128]{1,0:T(8,128)(2,1)S(1)}, bf16[128,128]{1,0:T(8,128)(2,1)}, u32[]{:S(2)}) %copy-start.3) | copy-done | bytes 32792
  4.1 0.0 copy-start.4
  4.1 0.8 %copy-done.4 = bf16[128,128]{1,0:T(8,128)(2,1)S(1)} copy-done((bf16[128,128]{1,0:T(8,128)(2,1)S(1)}, bf16[128,128]{1,0:T(8,128)(2,1)}, u32[]{:S(2)}) %copy-start.4) | copy-done | bytes 32792
  4.9 0.0 copy-start.5
  4.9 0.8 %copy-done.5 = bf16[128,128]{1,0:T(8,128)(2,1)S(1)} copy-done((bf16[128,128]{1,0:T(8,128)(2,1)S(1)}, bf16[128,128]{1,0:T(8,128)(2,1)}, u32[]{:S(2)}) %copy-start.5) | copy-done | bytes 32792
  5.6 0.0 copy-start.6
  5.6 0.7 %copy-done.6 = f32[8,128]{1,0:T(8,128)S(1)} copy-done((f32[8,128]{1,0:T(8,128)S(1)}, f32[8,128]{1,0:T(8,128)}, u32[]{:S(2)}) %copy-start.6) | copy-done | bytes 4120
  6.3 0.0 copy-start.7
  6.3 0.7 %copy-done.7 = f32[8]{0:T(128)S(1)} copy-done((f32[8]{0:T(128)S(1)}, f32[8]{0:T(128)}, u32[]{:S(2)}) %copy-start.7) | copy-done | bytes 56
  7.0 44.6 %shard_map.103 = (bf16[128,512]{1,0:T(8,128)(2,1)S(1)}, bf16[128,128]{1,0:T(8,128)(2,1)S(1)}, bf16[128,512]{1,0:T(8,128)(2,1)S(1)}) custom-call(bf16[128,512]{1,0:T(8,128)(2,1)S(1)} %copy-done, bf16[128,128]{1,0:T(8,128)(2,1)S(1)} %copy-done.3, bf16[128,512]{1,0:T(8,128)(2,1)S(1)} %copy-done.1, bf16[128,512]{1,0:T(8,128)(2,1)S(1)} %copy-done.2, ...), custom_call_target="tpu_custom_call" | custom-call | tf_op jit(solution)/shard_map/pallas_call | solution.py:379
  51.6 0.7 %copy.14 = bf16[128,512]{1,0:T(8,128)(2,1)} copy(bf16[128,512]{1,0:T(8,128)(2,1)S(1)} %get-tuple-element.6) | data formatting | bytes 262144
  52.3 0.6 %copy.15 = bf16[128,128]{1,0:T(8,128)(2,1)} copy(bf16[128,128]{1,0:T(8,128)(2,1)S(1)} %get-tuple-element.7) | data formatting | bytes 65536
  52.9 0.7 %copy.16 = bf16[128,512]{1,0:T(8,128)(2,1)} copy(bf16[128,512]{1,0:T(8,128)(2,1)S(1)} %get-tuple-element.8) | data formatting | bytes 262144
Async XLA Ops:
  0.6 0.9 %copy-start = (bf16[128,512]{1,0:T(8,128)(2,1)S(1)}, bf16[128,512]{1,0:T(8,128)(2,1)}, u32[]{:S(2)}) copy-start(bf16[128,512]{1,0:T(8,128)(2,1)} %q_ref.1) | copy-start | bytes 393220
  1.5 0.9 %copy-start.1 = (bf16[128,512]{1,0:T(8,128)(2,1)S(1)}, bf16[128,512]{1,0:T(8,128)(2,1)}, u32[]{:S(2)}) copy-start(bf16[128,512]{1,0:T(8,128)(2,1)} %do_ref.1) | copy-start | bytes 393220
  2.4 0.9 %copy-start.2 = (bf16[128,512]{1,0:T(8,128)(2,1)S(1)}, bf16[128,512]{1,0:T(8,128)(2,1)}, u32[]{:S(2)}) copy-start(bf16[128,512]{1,0:T(8,128)(2,1)} %dy_ref.1) | copy-start | bytes 393220
  3.3 0.8 %copy-start.3 = (bf16[128,128]{1,0:T(8,128)(2,1)S(1)}, bf16[128,128]{1,0:T(8,128)(2,1)}, u32[]{:S(2)}) copy-start(bf16[128,128]{1,0:T(8,128)(2,1)} %kv_ref.1) | copy-start | bytes 98308
  4.1 0.8 %copy-start.4 = (bf16[128,128]{1,0:T(8,128)(2,1)S(1)}, bf16[128,128]{1,0:T(8,128)(2,1)}, u32[]{:S(2)}) copy-start(bf16[128,128]{1,0:T(8,128)(2,1)} %b_ref.1) | copy-start | bytes 98308
  4.9 0.8 %copy-start.5 = (bf16[128,128]{1,0:T(8,128)(2,1)S(1)}, bf16[128,128]{1,0:T(8,128)(2,1)}, u32[]{:S(2)}) copy-start(bf16[128,128]{1,0:T(8,128)(2,1)} %c_ref.1) | copy-start | bytes 98308
  5.6 0.7 %copy-start.6 = (f32[8,128]{1,0:T(8,128)S(1)}, f32[8,128]{1,0:T(8,128)}, u32[]{:S(2)}) copy-start(f32[8,128]{1,0:T(8,128)} %dl_ref.1) | copy-start | bytes 12292
  6.3 0.7 %copy-start.7 = (f32[8]{0:T(128)S(1)}, f32[8]{0:T(128)}, u32[]{:S(2)}) copy-start(f32[8]{0:T(128)} %sg_ref.1) | copy-start | bytes 100

commit v2 on v1

--- a/solution.py
+++ b/solution.py
@@ -25,11 +25,12 @@
 
 
 def kernel(
-    n, hn, q_ref, kv_ref, do_ref, dy_ref, b_ref, c_ref, dl_ref, sg_ref,
+    n, hn, flat, q_hbm, kv_hbm, do_hbm, dy_hbm, b_hbm, c_hbm, dl_hbm, sg_ref,
     gq_ref, gkv_ref, gx_ref,
+    q_ref, kv_ref, do_ref, dy_ref, b_ref, c_ref, dl_ref,
     kv_all, q_st, q_t, do_st, do_t, score, dkv_out, dkv_in,
     st_out, st_in, dt_out, dt_in, inc_out, inc_in, dx, am_out, am_in, am2_out, am2_in,
-    kvs, kvr, dks, dkr, sts, str_, dts, dtr, ins, inr, ams, amr, am2s, am2r,
+    loads, fws, kvs, kvr, dks, dkr, sts, str_, dts, dtr, ins, inr, ams, amr, am2s, am2r,
 ):
     s = lax.axis_index("seq")
     h = lax.axis_index("head")
@@ -46,23 +47,52 @@
     sp = width // ssm_heads
     per = hd // sp
     chunk = 2 * rows
-
+    core = lax.rem(s, 2)
+    chip = s // 2
+    sibling = s + 1 - 2 * core
+
+    fetch = [
+        pltpu.make_async_copy(a, b, loads.at[i])
+        for i, (a, b) in enumerate((
+            (dl_hbm, dl_ref), (dy_hbm, dy_ref), (c_hbm, c_ref), (kv_hbm, kv_ref),
+            (b_hbm, b_ref), (q_hbm, q_ref), (do_hbm, do_ref),
+        ))
+    ]
+    for copy in fetch:
+        copy.start()
     barrier = pltpu.get_barrier_semaphore()
 
-    @pl.loop(0, n)
-    def _(d):
-        pl.semaphore_signal(barrier, inc=1, device_id=(d, mate), device_id_type=MESH)
-
-        @pl.when(d != s)
-        def _():
-            pl.semaphore_signal(barrier, inc=1, device_id=(d, h), device_id_type=MESH)
-
-    @pl.loop(0, hn)
-    def _(g):
-        @pl.when(jnp.logical_and(g != h, g != mate))
-        def _():
-            pl.semaphore_signal(barrier, inc=1, device_id=(s, g), device_id_type=MESH)
-
+    if flat:
+
+        @pl.loop(0, n)
+        def _(d):
+            @pl.loop(0, hn)
+            def _(g):
+                @pl.when(jnp.logical_or(d != s, g != h))
+                def _():
+                    pl.semaphore_signal(barrier, inc=1, device_id=(d, g), device_id_type=MESH)
+
+        greeted = n * hn - 1
+    else:
+
+        @pl.loop(0, n)
+        def _(d):
+            pl.semaphore_signal(barrier, inc=1, device_id=(d, mate), device_id_type=MESH)
+
+            @pl.when(d != s)
+            def _():
+                pl.semaphore_signal(barrier, inc=1, device_id=(d, h), device_id_type=MESH)
+
+        @pl.loop(0, hn)
+        def _(g):
+            @pl.when(jnp.logical_and(g != h, g != mate))
+            def _():
+                pl.semaphore_signal(barrier, inc=1, device_id=(s, g), device_id_type=MESH)
+
+        greeted = 2 * n - 1 + hn - 2
+
+    for copy in fetch[:4]:
+        copy.wait()
     kv_all[parity, s] = kv_ref[...]
 
     @pl.when(jnp.logical_and(lax.rem(s, 2) == 0, s + 1 < n))
@@ -96,7 +126,7 @@
         st_out[j] = state_t[j * srows : (j + 1) * srows]
     dt_out[...] = jnp.broadcast_to(jnp.exp(cum[:, rows - 1 : rows]), dt_out.shape)
 
-    pl.semaphore_wait(barrier, 2 * n - 1 + hn - 2)
+    pl.semaphore_wait(barrier, greeted)
 
     def kv_copy(d, g, source, kind):
         return pltpu.make_async_remote_copy(
@@ -105,6 +135,13 @@
             device_id=(d, g), device_id_type=MESH,
         )
 
+    def forward(source, kind):
+        return pltpu.make_async_remote_copy(
+            src_ref=kv_all.at[kind, source], dst_ref=kv_all.at[kind, source],
+            send_sem=fws.at[kind, source], recv_sem=kvr.at[kind, source],
+            device_id=(sibling, h), device_id_type=MESH,
+        )
+
     def st_copy(j, source):
         return pltpu.make_async_remote_copy(
             src_ref=st_out.at[j], dst_ref=st_in.at[source],
@@ -126,7 +163,16 @@
             device_id=(d, h), device_id_type=MESH,
         )
 
+    @pl.loop(chip + 1, n // 2)
+    def _(z):
+        kv_copy(2 * z + core, h, s, parity).start()
+        kv_copy(2 * z + core, mate, s, parity).start()
+
     kv_copy(s, mate, s, parity).start()
+
+    @pl.when(core == 0)
+    def _():
+        kv_copy(sibling, h, s, parity).start()
 
     @pl.loop(0, nh)
     def _(j):
@@ -135,11 +181,8 @@
             dt_copy(j, s).start()
             st_copy(j, s).start()
 
-    @pl.loop(s + 1, n)
-    def _(d):
-        kv_copy(d, h, s, parity).start()
-        kv_copy(d, mate, s, parity).start()
-
+    for copy in fetch[4:]:
+        copy.wait()
     for i in range(heads):
         q_i = q_ref[:, i * hd : (i + 1) * hd]
         d_i = do_ref[:, i * hd : (i + 1) * hd]
@@ -165,6 +208,45 @@
             )
         dx[:, i * hd : (i + 1) * hd] = total + gain * dy_i.astype(f32)
 
+    chunks = s // 2 + 1
+    key_i = lax.broadcasted_iota(jnp.int32, (chunk, cols), 0)
+    query_i = s * rows + lax.rem(lax.broadcasted_iota(jnp.int32, (1, cols), 1), rows)
+
+    def pass_on(kind):
+        @pl.loop(0, chip)
+        def _(z):
+            kv_copy(s, h, 2 * z + core, kind).wait_recv()
+            forward(2 * z + core, kind).start()
+
+        @pl.when(parity != kind)
+        def _():
+            kv_copy(s, h, s, kind).wait_recv()
+
+            @pl.when(core == 0)
+            def _():
+                forward(s, kind).start()
+
+    def await_kind(kind, j):
+        blk = 2 * j + 1 - core
+
+        @pl.when(blk < s)
+        def _():
+            kv_copy(s, h, blk, kind).wait_recv()
+
+    def load(kind, j):
+        return kv_all[kind, pl.ds(2 * j, 2)].reshape(chunk, hd)
+
+    def first(j, top):
+        await_kind(0, j)
+        sc = nn(load(0, j), q_t[...]) * scale
+        sc = jnp.where(key_i + j * chunk <= query_i, sc, -1e30)
+        score[j] = sc
+        return jnp.maximum(top, jnp.max(sc, axis=0, keepdims=True))
+
+    pass_on(0)
+    top = lax.fori_loop(0, chunks, first, jnp.full((1, cols), -1e30, f32))
+    pass_on(1)
+
     @pl.when(s < nh)
     def _():
         st_in[s] = st_out[jnp.minimum(s, nh - 1)]
@@ -192,30 +274,6 @@
         lax.fori_loop(0, n, one, jnp.zeros((srows, width), f32))
         inc_in[jnp.minimum(s, nh - 1)] = inc_out[s]
 
-    chunks = s // 2 + 1
-    key_i = lax.broadcasted_iota(jnp.int32, (chunk, cols), 0)
-    query_i = s * rows + lax.rem(lax.broadcasted_iota(jnp.int32, (1, cols), 1), rows)
-
-    def await_kind(kind, j):
-        for k in range(2):
-            blk = 2 * j + k
-
-            @pl.when(jnp.logical_and(blk <= s, jnp.logical_or(blk != s, parity != kind)))
-            def _():
-                kv_copy(s, h, blk, kind).wait_recv()
-
-    def load(kind, j):
-        return kv_all[kind, pl.ds(2 * j, 2)].reshape(chunk, hd)
-
-    def first(j, top):
-        await_kind(0, j)
-        sc = nn(load(0, j), q_t[...]) * scale
-        sc = jnp.where(key_i + j * chunk <= query_i, sc, -1e30)
-        score[j] = sc
-        return jnp.maximum(top, jnp.max(sc, axis=0, keepdims=True))
-
-    top = lax.fori_loop(0, chunks, first, jnp.full((1, cols), -1e30, f32))
-
     def second(j, total):
         e = jnp.exp(score[j] - top)
         score[j] = e
@@ -295,7 +353,23 @@
     sub = lax.broadcasted_iota(jnp.int32, am_out.shape, 0)
     mine = jnp.where(sub == 0, peak_q, jnp.where(sub == 1, peak_kv, peak_x))
     am_out[...] = mine
-    am_in[s] = mine
+    am_in[s * hn + h if flat else s] = mine
+
+    def am_all(d, g, e, f):
+        return pltpu.make_async_remote_copy(
+            src_ref=am_out, dst_ref=am_in.at[e * hn + f],
+            send_sem=ams.at[d * hn + g], recv_sem=amr.at[e * hn + f],
+            device_id=(d, g), device_id_type=MESH,
+        )
+
+    def all_others(act):
+        @pl.loop(0, n)
+        def _(d):
+            @pl.loop(0, hn)
+            def _(g):
+                @pl.when(jnp.logical_or(d != s, g != h))
+                def _():
+                    act(d, g)
 
     def am_copy(d, source):
         return pltpu.make_async_remote_copy(
@@ -318,14 +392,19 @@
             def _():
                 act(d)
 
-    each_other(n, s, lambda d: am_copy(d, s).start())
-    each_other(n, s, lambda d: am_copy(s, d).wait_recv())
-    column = jnp.max(am_in[...], axis=0)
-    am2_out[...] = column
-    am2_in[h] = column
-    each_other(hn, h, lambda g: am2_copy(g, h).start())
-    each_other(hn, h, lambda g: am2_copy(h, g).wait_recv())
-    inverse = 1.0 / (jnp.max(am2_in[...], axis=0) + epsilon)
+    if flat:
+        all_others(lambda d, g: am_all(d, g, s, h).start())
+        all_others(lambda d, g: am_all(s, h, d, g).wait_recv())
+        inverse = 1.0 / (jnp.max(am_in[...], axis=0) + epsilon)
+    else:
+        each_other(n, s, lambda d: am_copy(d, s).start())
+        each_other(n, s, lambda d: am_copy(s, d).wait_recv())
+        column = jnp.max(am_in[...], axis=0)
+        am2_out[...] = column
+        am2_in[h] = column
+        each_other(hn, h, lambda g: am2_copy(g, h).start())
+        each_other(hn, h, lambda g: am2_copy(h, g).wait_recv())
+        inverse = 1.0 / (jnp.max(am2_in[...], axis=0) + epsilon)
 
     scaled_q = dq_t * inverse[0:1, 0:1]
     for i in range(heads):
@@ -335,10 +414,20 @@
 
     kv_copy(s, mate, s, parity).wait_send()
 
-    @pl.loop(s + 1, n)
-    def _(d):
-        kv_copy(d, h, s, parity).wait_send()
-        kv_copy(d, mate, s, parity).wait_send()
+    @pl.when(core == 0)
+    def _():
+        kv_copy(sibling, h, s, parity).wait_send()
+        forward(s, 1 - parity).wait_send()
+
+    @pl.loop(chip + 1, n // 2)
+    def _(z):
+        kv_copy(2 * z + core, h, s, parity).wait_send()
+        kv_copy(2 * z + core, mate, s, parity).wait_send()
+
+    @pl.loop(0, chip)
+    def _(z):
+        forward(2 * z + core, 0).wait_send()
+        forward(2 * z + core, 1).wait_send()
 
     @pl.loop(0, nh)
     def _(j):
@@ -358,8 +447,21 @@
             def _():
                 dkv_copy(kind, blk, s, parity).wait_send()
 
-    each_other(n, s, lambda d: am_copy(d, s).wait_send())
-    each_other(hn, h, lambda g: am2_copy(g, h).wait_send())
+    if flat:
+        all_others(lambda d, g: am_all(d, g, s, h).wait_send())
+    else:
+        each_other(n, s, lambda d: am_copy(d, s).wait_send())
+        each_other(hn, h, lambda g: am2_copy(g, h).wait_send())
+
+
+def hand_over(a, b, c, x, y, z, sems):
+    copies = [
+        pltpu.make_async_copy(i, o, sems.at[k]) for k, (i, o) in enumerate(((a, x), (b, y), (c, z)))
+    ]
+    for copy in copies:
+        copy.start()
+    for copy in copies:
+        copy.wait()
 
 
 def on_device(queries, key_value, grad_out, ssm_grad, b_proj, c_proj, decay_log, skip_gain):
@@ -376,16 +478,23 @@
     vmem = pltpu.VMEM
     dma = pltpu.SemaphoreType.DMA
     full = pl.BlockSpec(memory_space=pltpu.VMEM)
-    return pl.pallas_call(
-        functools.partial(kernel, n, hn),
+    far = pl.BlockSpec(memory_space=pltpu.HBM)
+    flat = n * hn <= 64
+    groups = n * hn if flat else n
+    grads = pl.pallas_call(
+        functools.partial(kernel, n, hn, flat),
         out_shape=(
             jax.ShapeDtypeStruct(queries.shape, bf16),
             jax.ShapeDtypeStruct(key_value.shape, bf16),
             jax.ShapeDtypeStruct(ssm_grad.shape, bf16),
         ),
-        in_specs=[full] * 7 + [pl.BlockSpec(memory_space=pltpu.SMEM)],
+        in_specs=[far] * 7 + [pl.BlockSpec(memory_space=pltpu.SMEM)],
         out_specs=(full, full, full),
         scratch_shapes=[
+            *(
+                vmem(a.shape, a.dtype)
+                for a in (queries, key_value, grad_out, ssm_grad, b_proj, c_proj, decay_log)
+            ),
             vmem((2, n, rows, hd), bf16),
             vmem((cols, hd), bf16),
             vmem((hd, cols), bf16),
@@ -402,21 +511,30 @@
             vmem((nh, srows, width), bf16),
             vmem((rows, width), f32),
             vmem((8, hd), f32),
-            vmem((n, 8, hd), f32),
+            vmem((groups, 8, hd), f32),
             vmem((8, hd), f32),
             vmem((hn, 8, hd), f32),
+            dma((7,)), dma((2, n)),
             dma((2, n)), dma((2, n)),
             dma((2, n)), dma((n, 2)),
             dma((nh,)), dma((n,)),
             dma((nh,)), dma((n,)),
             dma((n,)), dma((nh,)),
-            dma((n,)), dma((n,)),
+            dma((groups,)), dma((groups,)),
             dma((hn,)), dma((hn,)),
         ],
         compiler_params=pltpu.CompilerParams(
-            collective_id=0, has_side_effects=True, vmem_limit_bytes=48 * 1024 * 1024
+            collective_id=0, has_side_effects=True, vmem_limit_bytes=56 * 1024 * 1024
         ),
     )(queries, key_value, grad_out, ssm_grad, b_proj, c_proj, decay_log, skip_gain)
+    return pl.pallas_call(
+        hand_over,
+        out_shape=tuple(jax.ShapeDtypeStruct(a.shape, a.dtype) for a in grads),
+        in_specs=[far] * 3,
+        out_specs=(far,) * 3,
+        scratch_shapes=[dma((3,))],
+        compiler_params=pltpu.CompilerParams(vmem_limit_bytes=56 * 1024 * 1024),
+    )(*grads)
 
 
 def solution(mesh):

time: 54 us -> 52.7 us (0.976)
  local copies, waits for them, and re-layouts: 8.24 us -> 0 us
  Pallas kernels: 44.6 us -> 51.9 us
    unnamed x19 -> x0, local copies, waits for them, and re-layouts: 8.24 us -> none
    pallas_call x1 -> x2, Pallas kernels: 44.6 us -> 51.9 us  [the longest x1 41.8 us: on_device(): pl.pallas_call(functools.partial(kernel, n, hn, flat), out_shape=(jax.Sha...]
where the time goes in v2:
time: 52.7 us; the launch traced here: 52.6 us
  Pallas kernels  51.9 us (98%)
  between operations  0.64 us (1%)
    pallas_call x1, Pallas kernels, on_device(): pl.pallas_call(functools.partial(kernel, n, hn, flat), out_shape=(jax.Sha...  41.8 us
    pallas_call x1, Pallas kernels, on_device(): pl.pallas_call(hand_over, out_shape=tuple((jax.ShapeDtypeStruct(a.shape,...  10.1 us

profile of v2, /device:TPU:0, one launch (start us, length us, event | category | flops | bytes accessed | tf_op | source)
XLA Modules:
  0.0 52.6 jit_solution(449225704071730677)
XLA Ops:
  0.6 41.8 %shard_map.103 = (bf16[128,512]{1,0:T(8,128)(2,1)}, bf16[128,128]{1,0:T(8,128)(2,1)}, bf16[128,512]{1,0:T(8,128)(2,1)}) custom-call(bf16[128,512]{1,0:T(8,128)(2,1)} %q_hbm.1, bf16[128,128]{1,0:T(8,128)(2,1)} %kv_hbm.1, bf16[128,512]{1,0:T(8,128)(2,1)} %do_hbm.1, bf16[128,512]{1,0:T(8,128)(2,1)} %dy_hbm.1, bf16[128,128]{1,0:T(8,128)(2,1)} %b_hbm.1, ...), custom_call_target="tpu_custom_call" | custom-call | tf_op jit(solution)/shard_map/pallas_call | solution.py:484
  42.5 10.1 %shard_map.104 = (bf16[128,512]{1,0:T(8,128)(2,1)}, bf16[128,128]{1,0:T(8,128)(2,1)}, bf16[128,512]{1,0:T(8,128)(2,1)}) custom-call(bf16[128,512]{1,0:T(8,128)(2,1)} %get-tuple-element.6.a, bf16[128,128]{1,0:T(8,128)(2,1)} %get-tuple-element.7.b, bf16[128,512]{1,0:T(8,128)(2,1)} %get-tuple-element.8.c), custom_call_target="tpu_custom_call" | custom-call | tf_op jit(solution)/shard_map/pallas_call | solution.py:530

commit v3 on v2

--- a/solution.py
+++ b/solution.py
@@ -25,12 +25,12 @@
 
 
 def kernel(
-    n, hn, flat, q_hbm, kv_hbm, do_hbm, dy_hbm, b_hbm, c_hbm, dl_hbm, sg_ref,
+    n, hn, q_hbm, kv_hbm, do_hbm, dy_hbm, b_hbm, c_hbm, dl_hbm, sg_ref,
     gq_ref, gkv_ref, gx_ref,
     q_ref, kv_ref, do_ref, dy_ref, b_ref, c_ref, dl_ref,
-    kv_all, q_st, q_t, do_st, do_t, score, dkv_out, dkv_in,
-    st_out, st_in, dt_out, dt_in, inc_out, inc_in, dx, am_out, am_in, am2_out, am2_in,
-    loads, fws, kvs, kvr, dks, dkr, sts, str_, dts, dtr, ins, inr, ams, amr, am2s, am2r,
+    kv_all, q_st, q_t, do_st, do_t, score, dkv_out, dkv_in, dkv_part, pair_in,
+    st_out, st_in, inc_out, inc_in, dx, am_out, am_in, am2_out, am2_in,
+    loads, fws, kvs, kvr, dks, dkr, prs, prr, sts, str_, ins, inr, ams, amr, am2s, am2r,
 ):
     s = lax.axis_index("seq")
     h = lax.axis_index("head")
@@ -62,34 +62,20 @@
         copy.start()
     barrier = pltpu.get_barrier_semaphore()
 
-    if flat:
-
-        @pl.loop(0, n)
-        def _(d):
-            @pl.loop(0, hn)
-            def _(g):
-                @pl.when(jnp.logical_or(d != s, g != h))
-                def _():
-                    pl.semaphore_signal(barrier, inc=1, device_id=(d, g), device_id_type=MESH)
-
-        greeted = n * hn - 1
-    else:
-
-        @pl.loop(0, n)
-        def _(d):
-            pl.semaphore_signal(barrier, inc=1, device_id=(d, mate), device_id_type=MESH)
-
-            @pl.when(d != s)
-            def _():
-                pl.semaphore_signal(barrier, inc=1, device_id=(d, h), device_id_type=MESH)
-
-        @pl.loop(0, hn)
-        def _(g):
-            @pl.when(jnp.logical_and(g != h, g != mate))
-            def _():
-                pl.semaphore_signal(barrier, inc=1, device_id=(s, g), device_id_type=MESH)
-
-        greeted = 2 * n - 1 + hn - 2
+    for k in range(1, n):
+        pl.semaphore_signal(
+            barrier, inc=1, device_id=(lax.rem(s + k, n), h), device_id_type=MESH
+        )
+    for k in range(0, n, 2):
+        pl.semaphore_signal(
+            barrier, inc=1, device_id=(lax.rem(s + k, n), mate), device_id_type=MESH
+        )
+    for k in range(2, hn):
+        g = lax.rem(base + k, hn)
+        pl.semaphore_signal(barrier, inc=1, device_id=(s, g), device_id_type=MESH)
+
+    def settle(ref, sem):
+        pltpu.make_async_copy(ref, ref, sem).wait()
 
     for copy in fetch[:4]:
         copy.wait()
@@ -123,10 +109,14 @@
     c_val = c_ref[...]
     state_t = nn(c_val.T, scaled).astype(bf16)
     for j in range(nh):
-        st_out[j] = state_t[j * srows : (j + 1) * srows]
-    dt_out[...] = jnp.broadcast_to(jnp.exp(cum[:, rows - 1 : rows]), dt_out.shape)
-
-    pl.semaphore_wait(barrier, greeted)
+        st_out[j, :, :width] = state_t[j * srows : (j + 1) * srows]
+    whole = jnp.broadcast_to(jnp.exp(cum[:, rows - 1 : rows]), (ssm_heads, hd))
+    high = whole.astype(bf16).astype(f32)
+    halves = jnp.concatenate([high, whole - high], axis=0).astype(bf16)
+    for j in range(nh):
+        st_out[j, :, width:] = halves
+
+    pl.semaphore_wait(barrier, n - 1 + n // 2 + hn - 2)
 
     def kv_copy(d, g, source, kind):
         return pltpu.make_async_remote_copy(
@@ -145,21 +135,14 @@
     def st_copy(j, source):
         return pltpu.make_async_remote_copy(
             src_ref=st_out.at[j], dst_ref=st_in.at[source],
-            send_sem=sts.at[j], recv_sem=str_.at[source],
+            send_sem=sts.at[0], recv_sem=str_.at[0],
             device_id=(j, h), device_id_type=MESH,
         )
 
-    def dt_copy(j, source):
-        return pltpu.make_async_remote_copy(
-            src_ref=dt_out, dst_ref=dt_in.at[source],
-            send_sem=dts.at[j], recv_sem=dtr.at[source],
-            device_id=(j, h), device_id_type=MESH,
-        )
-
     def inc_copy(d, source):
         return pltpu.make_async_remote_copy(
             src_ref=inc_out.at[d], dst_ref=inc_in.at[source],
-            send_sem=ins.at[d], recv_sem=inr.at[source],
+            send_sem=ins.at[0], recv_sem=inr.at[0],
             device_id=(d, h), device_id_type=MESH,
         )
 
@@ -178,7 +161,6 @@
     def _(j):
         @pl.when(j != s)
         def _():
-            dt_copy(j, s).start()
             st_copy(j, s).start()
 
     for copy in fetch[4:]:
@@ -250,7 +232,7 @@
     @pl.when(s < nh)
     def _():
         st_in[s] = st_out[jnp.minimum(s, nh - 1)]
-        dt_in[s] = dt_out[...]
+        settle(st_in.at[pl.ds(0, n - 1)], str_.at[0])
 
         def one(step, inc):
             i = n - 1 - step
@@ -259,17 +241,16 @@
             @pl.when(i != s)
             def _():
                 inc_copy(i, s).start()
-                st_copy(jnp.minimum(s, nh - 1), i).wait_recv()
-                dt_copy(jnp.minimum(s, nh - 1), i).wait_recv()
-
-            d = dt_in[i]
+
+            d = st_in[i, :, width:].astype(f32)
+            d = d[:ssm_heads] + d[ssm_heads:]
             parts = []
             for a in range(ssm_heads // per):
                 v = d[a * per : a * per + 1]
                 for k in range(1, per):
                     v = jnp.where(lane == k, d[a * per + k : a * per + k + 1], v)
                 parts.append(v)
-            return st_in[i].astype(f32) + jnp.concatenate(parts, axis=1) * inc
+            return st_in[i, :, :width].astype(f32) + jnp.concatenate(parts, axis=1) * inc
 
         lax.fori_loop(0, n, one, jnp.zeros((srows, width), f32))
         inc_in[jnp.minimum(s, nh - 1)] = inc_out[s]
@@ -284,22 +265,36 @@
 
     def dkv_copy(kind, blk, source, member):
         return pltpu.make_async_remote_copy(
-            src_ref=dkv_out.at[kind, blk], dst_ref=dkv_in.at[source, member],
+            src_ref=dkv_out.at[kind, 2 * blk + core], dst_ref=dkv_in.at[source, member],
             send_sem=dks.at[kind, blk], recv_sem=dkr.at[source, member],
-            device_id=(blk, base + kind), device_id_type=MESH,
-        )
-
-    def other(kind, blk):
-        return jnp.logical_and(blk <= s, jnp.logical_or(blk != s, parity != kind))
+            device_id=(2 * blk + core, base + kind), device_id_type=MESH,
+        )
+
+    def pair_copy(kind, j):
+        return pltpu.make_async_remote_copy(
+            src_ref=dkv_out.at[kind, 2 * j + 1 - core], dst_ref=pair_in.at[kind, j],
+            send_sem=prs.at[kind, j], recv_sem=prr.at[kind, j],
+            device_id=(sibling, h), device_id_type=MESH,
+        )
+
+    def other(kind, z):
+        return jnp.logical_or(z != chip, parity != kind)
+
+    def pair_sum(kind, j):
+        pair_copy(kind, j).wait_recv()
+        both = dkv_part[kind, j] + pair_in[kind, j].astype(f32)
+        dkv_out[kind, 2 * j + core] = both.astype(bf16)
+
+        @pl.when(other(kind, j))
+        def _():
+            dkv_copy(kind, j, chip, parity).start()
 
     def send_grads(kind, j, val):
-        for k in range(2):
-            blk = 2 * j + k
-            dkv_out[kind, blk] = val[k * rows : (k + 1) * rows].astype(bf16)
-
-            @pl.when(other(kind, blk))
-            def _():
-                dkv_copy(kind, blk, s, parity).start()
+        low, high = val[:rows], val[rows:]
+        first_core = jnp.full((1, hd), core, jnp.int32) == 0
+        dkv_out[kind, 2 * j + 1 - core] = jnp.where(first_core, high, low).astype(bf16)
+        pair_copy(kind, j).start()
+        dkv_part[kind, j] = jnp.where(first_core, low, high)
 
     def third(j, out):
         await_kind(1, j)
@@ -316,15 +311,22 @@
         dp = nn(load(1, j), do_t[...])
         ds = (score[j] * (dp - delta)).astype(bf16)
         send_grads(0, j, nn(ds, q_st[...]) * scale)
+        pair_sum(1, j)
         return dq + nn(load(0, j).T, ds)
 
     dq_t = lax.fori_loop(0, chunks, fourth, jnp.zeros((hd, cols), f32)) * scale
 
-    @pl.loop(0, nh)
+    @pl.loop(0, chunks)
     def _(j):
-        @pl.when(j != s)
-        def _():
-            inc_copy(s, j).wait_recv()
+        pair_sum(0, j)
+
+    @pl.when(s < nh)
+    def _():
+        settle(inc_in.at[pl.ds(0, nh - 1)], inr.at[0])
+
+    @pl.when(s >= nh)
+    def _():
+        settle(inc_in, inr.at[0])
 
     carried = nn(b_ref[...], inc_in[...].reshape(nh * srows, width))
     tail = spread(jnp.exp(cum_t[rows - 1 : rows, :] - cum_t))
@@ -339,72 +341,46 @@
 
     def add_source(i, acc):
         for m in range(2):
-            @pl.when(jnp.logical_or(i != s, parity != m))
+            @pl.when(jnp.logical_or(i != chip, parity != m))
             def _():
-                dkv_copy(parity, s, i, m).wait_recv()
+                dkv_copy(parity, chip, i, m).wait_recv()
 
             acc = acc + dkv_in[i, m].astype(f32)
         return acc
 
-    dkv_in[s, parity] = dkv_out[parity, s]
-    kv_grad = lax.fori_loop(s, n, add_source, jnp.zeros((rows, hd), f32))
+    dkv_in[chip, parity] = dkv_out[parity, s]
+    kv_grad = lax.fori_loop(chip, n // 2, add_source, jnp.zeros((rows, hd), f32))
     peak_kv = peak(kv_grad)
 
     sub = lax.broadcasted_iota(jnp.int32, am_out.shape, 0)
     mine = jnp.where(sub == 0, peak_q, jnp.where(sub == 1, peak_kv, peak_x))
     am_out[...] = mine
-    am_in[s * hn + h if flat else s] = mine
-
-    def am_all(d, g, e, f):
-        return pltpu.make_async_remote_copy(
-            src_ref=am_out, dst_ref=am_in.at[e * hn + f],
-            send_sem=ams.at[d * hn + g], recv_sem=amr.at[e * hn + f],
-            device_id=(d, g), device_id_type=MESH,
-        )
-
-    def all_others(act):
-        @pl.loop(0, n)
-        def _(d):
-            @pl.loop(0, hn)
-            def _(g):
-                @pl.when(jnp.logical_or(d != s, g != h))
-                def _():
-                    act(d, g)
+    am_in[s] = mine
 
     def am_copy(d, source):
         return pltpu.make_async_remote_copy(
             src_ref=am_out, dst_ref=am_in.at[source],
-            send_sem=ams.at[d], recv_sem=amr.at[source],
+            send_sem=ams.at[0], recv_sem=amr.at[0],
             device_id=(d, h), device_id_type=MESH,
         )
 
     def am2_copy(g, source):
         return pltpu.make_async_remote_copy(
             src_ref=am2_out, dst_ref=am2_in.at[source],
-            send_sem=am2s.at[g], recv_sem=am2r.at[source],
+            send_sem=am2s.at[0], recv_sem=am2r.at[0],
             device_id=(s, g), device_id_type=MESH,
         )
 
-    def each_other(count, me, act):
-        @pl.loop(0, count)
-        def _(d):
-            @pl.when(d != me)
-            def _():
-                act(d)
-
-    if flat:
-        all_others(lambda d, g: am_all(d, g, s, h).start())
-        all_others(lambda d, g: am_all(s, h, d, g).wait_recv())
-        inverse = 1.0 / (jnp.max(am_in[...], axis=0) + epsilon)
-    else:
-        each_other(n, s, lambda d: am_copy(d, s).start())
-        each_other(n, s, lambda d: am_copy(s, d).wait_recv())
-        column = jnp.max(am_in[...], axis=0)
-        am2_out[...] = column
-        am2_in[h] = column
-        each_other(hn, h, lambda g: am2_copy(g, h).start())
-        each_other(hn, h, lambda g: am2_copy(h, g).wait_recv())
-        inverse = 1.0 / (jnp.max(am2_in[...], axis=0) + epsilon)
+    for k in range(1, n):
+        am_copy(lax.rem(s + k, n), s).start()
+    settle(am_in.at[pl.ds(0, n - 1)], amr.at[0])
+    column = jnp.max(am_in[...], axis=0)
+    am2_out[...] = column
+    am2_in[h] = column
+    for k in range(1, hn):
+        am2_copy(lax.rem(h + k, hn), h).start()
+    settle(am2_in.at[pl.ds(0, hn - 1)], am2r.at[0])
+    inverse = 1.0 / (jnp.max(am2_in[...], axis=0) + epsilon)
 
     scaled_q = dq_t * inverse[0:1, 0:1]
     for i in range(heads):
@@ -429,39 +405,40 @@
         forward(2 * z + core, 0).wait_send()
         forward(2 * z + core, 1).wait_send()
 
-    @pl.loop(0, nh)
-    def _(j):
-        @pl.when(j != s)
-        def _():
-            st_copy(j, s).wait_send()
-            dt_copy(j, s).wait_send()
-
     @pl.when(s < nh)
     def _():
-        each_other(n, s, lambda d: inc_copy(d, s).wait_send())
-
-    @pl.loop(0, s + 1)
-    def _(blk):
+        settle(st_out.at[pl.ds(0, nh - 1)], sts.at[0])
+        settle(inc_out.at[pl.ds(0, n - 1)], ins.at[0])
+
+    @pl.when(s >= nh)
+    def _():
+        settle(st_out, sts.at[0])
+
+    @pl.loop(0, chunks)
+    def _(z):
         for kind in range(2):
-            @pl.when(other(kind, blk))
+            pair_copy(kind, z).wait_send()
+
+            @pl.when(other(kind, z))
             def _():
-                dkv_copy(kind, blk, s, parity).wait_send()
-
-    if flat:
-        all_others(lambda d, g: am_all(d, g, s, h).wait_send())
-    else:
-        each_other(n, s, lambda d: am_copy(d, s).wait_send())
-        each_other(hn, h, lambda g: am2_copy(g, h).wait_send())
-
-
-def hand_over(a, b, c, x, y, z, sems):
-    copies = [
-        pltpu.make_async_copy(i, o, sems.at[k]) for k, (i, o) in enumerate(((a, x), (b, y), (c, z)))
+                dkv_copy(kind, z, chip, parity).wait_send()
+
+    settle(am_in.at[pl.ds(0, n - 1)], ams.at[0])
+    settle(am2_in.at[pl.ds(0, hn - 1)], am2s.at[0])
+
+
+def hand_over(a, b, c, x, y, z, u, v, w, in_sems, out_sems):
+    hops = [
+        (pltpu.make_async_copy(i, m, in_sems.at[k]), pltpu.make_async_copy(m, o, out_sems.at[k]))
+        for k, (i, m, o) in enumerate(((a, u, x), (b, v, y), (c, w, z)))
     ]
-    for copy in copies:
-        copy.start()
-    for copy in copies:
-        copy.wait()
+    for hop in hops:
+        hop[0].start()
+    for hop in hops:
+        hop[0].wait()
+        hop[1].start()
+    for hop in hops:
+        hop[1].wait()
 
 
 def on_device(queries, key_value, grad_out, ssm_grad, b_proj, c_proj, decay_log, skip_gain):
@@ -479,10 +456,8 @@
     dma = pltpu.SemaphoreType.DMA
     full = pl.BlockSpec(memory_space=pltpu.VMEM)
     far = pl.BlockSpec(memory_space=pltpu.HBM)
-    flat = n * hn <= 64
-    groups = n * hn if flat else n
     grads = pl.pallas_call(
-        functools.partial(kernel, n, hn, flat),
+        functools.partial(kernel, n, hn),
         out_shape=(
             jax.ShapeDtypeStruct(queries.shape, bf16),
             jax.ShapeDtypeStruct(key_value.shape, bf16),
@@ -502,26 +477,23 @@
             vmem((hd, cols), bf16),
             vmem((n // 2, 2 * rows, cols), f32),
             vmem((2, n, rows, hd), bf16),
-            vmem((n, 2, rows, hd), bf16),
-            vmem((nh, srows, width), bf16),
-            vmem((n, srows, width), bf16),
-            vmem((ssm_heads, hd), f32),
-            vmem((n, ssm_heads, hd), f32),
+            vmem((n // 2, 2, rows, hd), bf16),
+            vmem((2, n // 2, rows, hd), f32),
+            vmem((2, n // 2, rows, hd), bf16),
+            vmem((nh, srows, width + hd), bf16),
+            vmem((n, srows, width + hd), bf16),
             vmem((n, srows, width), bf16),
             vmem((nh, srows, width), bf16),
             vmem((rows, width), f32),
             vmem((8, hd), f32),
-            vmem((groups, 8, hd), f32),
+            vmem((n, 8, hd), f32),
             vmem((8, hd), f32),
             vmem((hn, 8, hd), f32),
             dma((7,)), dma((2, n)),
             dma((2, n)), dma((2, n)),
-            dma((2, n)), dma((n, 2)),
-            dma((nh,)), dma((n,)),
-            dma((nh,)), dma((n,)),
-            dma((n,)), dma((nh,)),
-            dma((groups,)), dma((groups,)),
-            dma((hn,)), dma((hn,)),
+            dma((2, n // 2)), dma((n // 2, 2)),
+            dma((2, n // 2)), dma((2, n // 2)),
+            *(dma((1,)) for _ in range(8)),
         ],
         compiler_params=pltpu.CompilerParams(
             collective_id=0, has_side_effects=True, vmem_limit_bytes=56 * 1024 * 1024
@@ -532,7 +504,7 @@
         out_shape=tuple(jax.ShapeDtypeStruct(a.shape, a.dtype) for a in grads),
         in_specs=[far] * 3,
         out_specs=(far,) * 3,
-        scratch_shapes=[dma((3,))],
+        scratch_shapes=[*(vmem(a.shape, a.dtype) for a in grads), dma((3,)), dma((3,))],
         compiler_params=pltpu.CompilerParams(vmem_limit_bytes=56 * 1024 * 1024),
     )(*grads)
 

time: 52.7 us -> 41 us (0.78)
  Pallas kernels: 51.9 us -> 40.2 us
    pallas_call x1, Pallas kernels: 10.1 us -> 1.69 us  [on_device(): pl.pallas_call(hand_over, out_shape=tuple((jax.ShapeDtypeStruct(a.shape,...]
    pallas_call x1, Pallas kernels: 41.8 us -> 38.5 us  [on_device(): pl.pallas_call(functools.partial(kernel, n, hn), out_shape=(jax.ShapeDtyp...]
where the time goes in v3:
time: 41 us; the launch traced here: 40.8 us
  Pallas kernels  40.2 us (98%)
  between operations  0.64 us (2%)
    pallas_call x1, Pallas kernels, on_device(): pl.pallas_call(functools.partial(kernel, n, hn), out_shape=(jax.ShapeDtyp...  38.5 us
    pallas_call x1, Pallas kernels, on_device(): pl.pallas_call(hand_over, out_shape=tuple((jax.ShapeDtypeStruct(a.shape,...  1.69 us

profile of v3, /device:TPU:0, one launch (start us, length us, event | category | flops | bytes accessed | tf_op | source)
XLA Modules:
  0.0 40.8 jit_solution(12697452431300545866)
XLA Ops:
  0.6 38.5 %shard_map.103 = (bf16[128,512]{1,0:T(8,128)(2,1)}, bf16[128,128]{1,0:T(8,128)(2,1)}, bf16[128,512]{1,0:T(8,128)(2,1)}) custom-call(bf16[128,512]{1,0:T(8,128)(2,1)} %q_hbm.1, bf16[128,128]{1,0:T(8,128)(2,1)} %kv_hbm.1, bf16[128,512]{1,0:T(8,128)(2,1)} %do_hbm.1, bf16[128,512]{1,0:T(8,128)(2,1)} %dy_hbm.1, bf16[128,128]{1,0:T(8,128)(2,1)} %b_hbm.1, ...), custom_call_target="tpu_custom_call" | custom-call | tf_op jit(solution)/shard_map/pallas_call | solution.py:459
  39.1 1.7 %shard_map.104 = (bf16[128,512]{1,0:T(8,128)(2,1)}, bf16[128,128]{1,0:T(8,128)(2,1)}, bf16[128,512]{1,0:T(8,128)(2,1)}) custom-call(bf16[128,512]{1,0:T(8,128)(2,1)} %get-tuple-element.6.a, bf16[128,128]{1,0:T(8,128)(2,1)} %get-tuple-element.7.b, bf16[128,512]{1,0:T(8,128)(2,1)} %get-tuple-element.8.c), custom_call_target="tpu_custom_call" | custom-call | tf_op jit(solution)/shard_map/pallas_call | solution.py:502

commit v4 on v3

--- a/solution.py
+++ b/solution.py
@@ -227,8 +227,6 @@
 
     pass_on(0)
     top = lax.fori_loop(0, chunks, first, jnp.full((1, cols), -1e30, f32))
-    pass_on(1)
-
     @pl.when(s < nh)
     def _():
         st_in[s] = st_out[jnp.minimum(s, nh - 1)]
@@ -254,6 +252,8 @@
 
         lax.fori_loop(0, n, one, jnp.zeros((srows, width), f32))
         inc_in[jnp.minimum(s, nh - 1)] = inc_out[s]
+
+    pass_on(1)
 
     def second(j, total):
         e = jnp.exp(score[j] - top)

time: 41 us -> 41.1 us (level)
  no operation moved by 1% of the time
where the time goes in v4:
time: 41.1 us; the launch traced here: 40.9 us
  Pallas kernels  40.2 us (98%)
  between operations  0.64 us (2%)
    pallas_call x1, Pallas kernels, on_device(): pl.pallas_call(functools.partial(kernel, n, hn), out_shape=(jax.ShapeDtyp...  38.5 us
    pallas_call x1, Pallas kernels, on_device(): pl.pallas_call(hand_over, out_shape=tuple((jax.ShapeDtypeStruct(a.shape,...  1.69 us

profile of v4, /device:TPU:0, one launch (start us, length us, event | category | flops | bytes accessed | tf_op | source)
XLA Modules:
  0.0 40.9 jit_solution(4148054317144733443)
XLA Ops:
  0.6 38.5 %shard_map.103 = (bf16[128,512]{1,0:T(8,128)(2,1)}, bf16[128,128]{1,0:T(8,128)(2,1)}, bf16[128,512]{1,0:T(8,128)(2,1)}) custom-call(bf16[128,512]{1,0:T(8,128)(2,1)} %q_hbm.1, bf16[128,128]{1,0:T(8,128)(2,1)} %kv_hbm.1, bf16[128,512]{1,0:T(8,128)(2,1)} %do_hbm.1, bf16[128,512]{1,0:T(8,128)(2,1)} %dy_hbm.1, bf16[128,128]{1,0:T(8,128)(2,1)} %b_hbm.1, ...), custom_call_target="tpu_custom_call" | custom-call | tf_op jit(solution)/shard_map/pallas_call | solution.py:459
  39.2 1.7 %shard_map.104 = (bf16[128,512]{1,0:T(8,128)(2,1)}, bf16[128,128]{1,0:T(8,128)(2,1)}, bf16[128,512]{1,0:T(8,128)(2,1)}) custom-call(bf16[128,512]{1,0:T(8,128)(2,1)} %get-tuple-element.6.a, bf16[128,128]{1,0:T(8,128)(2,1)} %get-tuple-element.7.b, bf16[128,512]{1,0:T(8,128)(2,1)} %get-tuple-element.8.c), custom_call_target="tpu_custom_call" | custom-call | tf_op jit(solution)/shard_map/pallas_call | solution.py:502
